TPU v7x, 512 devices: a whole 4x4x16 slice. The times are simulated.
512 devices in a mesh: seq: 64 (over y, z), chan: 8 (over x, core).
Axes of the slice: x: 4, y: 4, z: 16, core: 2. Of those that a mesh axis runs over, the one named last changes fastest.
Arguments:
- x1: bfloat16 [8192, 4096], P('seq', 'chan'), may hold values from -6 to 6
- x2: bfloat16 [8192, 4096], P('seq', 'chan'), may hold values from -6 to 6
- value: bfloat16 [8192, 4096], P('seq', 'chan'), may hold values from -6 to 6
- out_grad: bfloat16 [8192, 4096], P('seq', 'chan'), may hold values from -6 to 6
- short_weight: float32 [3, 4096], P(None, 'chan'), may hold values from -3.5 to 3.5
- coef: float32 [64, 4096], P(None, 'chan'), may hold values from -0.75 to 0.75
- rate: float32 [64], replicated, may hold values from 0.2 to 273.06667, as said below
Outputs:
- layer_output: bfloat16 [8192, 4096], P('seq', 'chan')
- grad_x1: bfloat16 [8192, 4096], P('seq', 'chan')
- grad_value: bfloat16 [8192, 4096], P('seq', 'chan')
- grad_coef: float32 [64, 4096], P(None, 'chan')
- grad_rate: float32 [64], replicated
Inputs may be any that keep to these rules, and one draw needn't show every extreme that they name: `rate`: decay rates of the basis functions, per 8192 positions.
All inputs are finite; a program needn't handle non-finite values.
Results may differ from a plain program's by a relative error of at most 0.011.
Values may be sent and summed in bfloat16 or wider, within the bound.
No kernel may reach another device: no remote copies, remote signals or barrier semaphores. Data moves between devices by JAX's collectives and lax.ppermute only.
A program may use at most 64 MiB of HBM per device.

v0:
```python
import math
import jax
import jax.numpy as jnp
from jax import lax
from jax.sharding import PartitionSpec as P

highest = lax.Precision.HIGHEST


def from_behind(shard, axis, by):
    peers = lax.axis_size(axis)
    pairs = [(i, i + by) for i in range(peers) if 0 <= i + by < peers]
    return lax.ppermute(shard, axis, pairs)


def angles(index, period):
    return 2.0 * math.pi / period * (index % period).astype(jnp.float32)


def basis_pair(rate, start, count, length):
    position = start + jnp.arange(count, dtype=jnp.int32)
    index = jnp.arange(rate.shape[0], dtype=jnp.int32)
    cycles = (index // 2 + 1) * (index // 2 + 1)
    turned = position[:, None] * cycles[None, :] % length
    angle = 2.0 * math.pi / length * turned.astype(jnp.float32)
    wave = jnp.where(index[None, :] % 2 == 0, jnp.cos(angle), jnp.sin(angle))
    scaled = position.astype(jnp.float32)[:, None] / length
    envelope = jnp.sqrt(2.0 * rate / length)[None, :] * jnp.exp(-rate[None, :] * scaled)
    phi = envelope * wave
    psi = (0.5 / rate[None, :] - scaled) * phi
    return (phi, psi)


def row_tables(rows):
    every = jnp.arange(rows, dtype=jnp.int32)
    angle = angles(every[:, None] * every[None, :], rows)
    return (jnp.cos(angle), jnp.sin(angle))


def forward_transform(columns):
    shards = lax.axis_size("seq")
    place = lax.axis_index("seq")
    rows = columns.shape[0]
    slab = rows // shards
    width = columns.shape[1]
    received = lax.all_to_all(
        columns.reshape(shards, slab, width), "seq", split_axis=0, concat_axis=0, tiled=True
    )
    flat = received.reshape(shards, slab * width)
    freq_low = jnp.arange(2 * shards, dtype=jnp.int32)
    sources = jnp.arange(shards, dtype=jnp.int32)
    first = angles(freq_low[:, None] * sources[None, :], 2 * shards)
    real_a = jnp.dot(jnp.cos(first), flat, precision=highest).reshape(2 * shards, slab, width)
    imag_a = -jnp.dot(jnp.sin(first), flat, precision=highest).reshape(2 * shards, slab, width)
    local_rows = place * slab + jnp.arange(slab, dtype=jnp.int32)
    twist = angles(freq_low[:, None] * local_rows[None, :], 2 * shards * rows)
    cos_t = jnp.cos(twist)[:, :, None]
    sin_t = jnp.sin(twist)[:, :, None]
    real_b = real_a * cos_t + imag_a * sin_t
    imag_b = imag_a * cos_t - real_a * sin_t
    gathered = lax.all_to_all(
        jnp.stack([real_b, imag_b]), "seq", split_axis=1, concat_axis=2, tiled=True
    )
    cos_m, sin_m = row_tables(rows)
    real_x = jnp.einsum("fm,rmk->rfk", cos_m, gathered[0], precision=highest) + jnp.einsum(
        "fm,rmk->rfk", sin_m, gathered[1], precision=highest
    )
    imag_x = jnp.einsum("fm,rmk->rfk", cos_m, gathered[1], precision=highest) - jnp.einsum(
        "fm,rmk->rfk", sin_m, gathered[0], precision=highest
    )
    return (real_x, imag_x)


def inverse_transform(real_x, imag_x):
    shards = lax.axis_size("seq")
    place = lax.axis_index("seq")
    rows = real_x.shape[1]
    slab = rows // shards
    width = real_x.shape[2]
    total = 2 * shards * rows
    cos_m, sin_m = row_tables(rows)
    real_b = jnp.einsum("mf,rfk->rmk", cos_m, real_x, precision=highest) - jnp.einsum(
        "mf,rfk->rmk", sin_m, imag_x, precision=highest
    )
    imag_b = jnp.einsum("mf,rfk->rmk", cos_m, imag_x, precision=highest) + jnp.einsum(
        "mf,rfk->rmk", sin_m, real_x, precision=highest
    )
    freq_low = place * 2 + jnp.arange(2, dtype=jnp.int32)
    every = jnp.arange(rows, dtype=jnp.int32)
    twist = angles(freq_low[:, None] * every[None, :], total)
    cos_t = jnp.cos(twist)[:, :, None]
    sin_t = jnp.sin(twist)[:, :, None]
    real_c = real_b * cos_t - imag_b * sin_t
    imag_c = real_b * sin_t + imag_b * cos_t
    spread = lax.all_to_all(
        jnp.stack([real_c, imag_c]), "seq", split_axis=2, concat_axis=1, tiled=True
    )
    targets = jnp.arange(shards, dtype=jnp.int32)
    all_low = jnp.arange(2 * shards, dtype=jnp.int32)
    last = angles(targets[:, None] * all_low[None, :], 2 * shards)
    real_flat = spread[0].reshape(2 * shards, slab * width)
    imag_flat = spread[1].reshape(2 * shards, slab * width)
    signal = (
        jnp.dot(jnp.cos(last), real_flat, precision=highest)
        - jnp.dot(jnp.sin(last), imag_flat, precision=highest)
    ) / total
    returned = lax.all_to_all(
        signal.reshape(shards, slab, width), "seq", split_axis=0, concat_axis=1, tiled=True
    )
    return returned.reshape(rows, width)


def per_device(x1, x2, value, out_grad, short_weight, coef, rate):
    shards = lax.axis_size("seq")
    place = lax.axis_index("seq")
    rows = x1.shape[0]
    chans = x1.shape[1]
    length = rows * shards
    taps = short_weight.shape[0]
    prior = from_behind(value[rows - (taps - 1) :], "seq", 1)
    extended = jnp.concatenate([prior, value], axis=0).astype(jnp.float32)
    mixed = short_weight[0][None, :] * extended[taps - 1 : taps - 1 + rows]
    for shift_k in range(1, taps):
        mixed = (
            mixed
            + short_weight[shift_k][None, :]
            * extended[taps - 1 - shift_k : taps - 1 - shift_k + rows]
        )
    first = x1.astype(jnp.float32)
    second = x2.astype(jnp.float32)
    gated = (first * mixed).astype(jnp.bfloat16)
    grad_conv = (out_grad.astype(jnp.float32) * second).astype(jnp.bfloat16)
    phi, psi = basis_pair(rate, place * rows, rows, length)
    kernel = jnp.dot(phi, coef, precision=highest)
    columns = jnp.concatenate(
        [gated.astype(jnp.float32), grad_conv.astype(jnp.float32), kernel], axis=1
    )
    real_x, imag_x = forward_transform(columns)
    real_u, imag_u = (real_x[:, :, :chans], imag_x[:, :, :chans])
    real_d, imag_d = (real_x[:, :, chans : 2 * chans], imag_x[:, :, chans : 2 * chans])
    real_h, imag_h = (real_x[:, :, 2 * chans :], imag_x[:, :, 2 * chans :])
    real_z = real_u * real_h - imag_u * imag_h
    imag_z = real_u * imag_h + imag_u * real_h
    real_g = real_h * real_d + imag_h * imag_d
    imag_g = real_h * imag_d - imag_h * real_d
    real_f = real_u * real_d + imag_u * imag_d
    imag_f = real_u * imag_d - imag_u * real_d
    signals = inverse_transform(
        jnp.concatenate([real_z, real_g, real_f], axis=2),
        jnp.concatenate([imag_z, imag_g, imag_f], axis=2),
    )
    conv = signals[:, :chans]
    grad_gated = signals[:, chans : 2 * chans]
    grad_filter = signals[:, 2 * chans :]
    coef_part = jnp.dot(phi.T, grad_filter, precision=highest) * length ** (-0.5)
    rate_part = jnp.sum(psi * jnp.dot(grad_filter, coef.T, precision=highest), axis=0)
    grad_coef = lax.psum(coef_part, "seq")
    rate_sum = lax.psum(rate_part, ("seq", "chan"))
    grad_rate = rate_sum * (length * chans * lax.axis_size("chan")) ** (-0.5)
    out_y = (second * conv).astype(jnp.bfloat16)
    grad_x1 = (grad_gated * mixed).astype(jnp.bfloat16)
    grad_mixed = grad_gated * first
    later = from_behind(grad_mixed[: taps - 1], "seq", -1)
    tail = jnp.concatenate([grad_mixed, later], axis=0)
    back = short_weight[0][None, :] * tail[0:rows]
    for shift_k in range(1, taps):
        back = back + short_weight[shift_k][None, :] * tail[shift_k : shift_k + rows]
    grad_value = back.astype(jnp.bfloat16)
    return (out_y, grad_x1, grad_value, grad_coef, grad_rate)


def solution(mesh):
    return jax.shard_map(
        per_device,
        mesh=mesh,
        in_specs=(
            P("seq", "chan"),
            P("seq", "chan"),
            P("seq", "chan"),
            P("seq", "chan"),
            P(None, "chan"),
            P(None, "chan"),
            P(),
        ),
        out_specs=(P("seq", "chan"), P("seq", "chan"), P("seq", "chan"), P(None, "chan"), P()),
        check_vma=False,
    )
```

profile of v0, /device:TPU:2, one launch (start us, length us, event | category | flops | bytes accessed | tf_op | source)
XLA Modules:
  0.0 738.9 jit_solution(4605748889626512701)
XLA Ops:
  7.9 3.8 collective-permute-start
  18.1 18.9 %all-to-all-start = ((f32[64,2,1536]{2,1,0:T(2,128)}), f32[64,2,1536]{2,1,0:T(2,128)S(1)}, u32[]{:S(2)}, u32[]{:S(2)}) async-start(f32[64,2,1536]{2,1,0:T(2,128)} %reshape.196), calls=%async_computation | async-start | bytes 1572864 | tf_op jit(solution)/shard_map/all_to_all | solution.py:46
  37.6 40.5 %all-to-all-done = f32[64,2,1536]{2,1,0:T(2,128)S(1)} async-done(((f32[64,2,1536]{2,1,0:T(2,128)}), f32[64,2,1536]{2,1,0:T(2,128)S(1)}, u32[]{:S(2)}, u32[]{:S(2)}) %all-to-all-start) | async-done | bytes 786464 | tf_op jit(solution)/shard_map/all_to_all | solution.py:46
  79.7 1.9 add_bitcast_fusion.1
  81.8 4.1 copy.26
  85.8 7.1 all-to-all-start.1
  92.9 11.9 %all-reduce.2.cloned.1.call-start = ((), (), s32[]{:S(2)}) async-start(), calls=%async_computation.4 | async-start | bytes 262144 | tf_op jit(solution)/shard_map/psum | solution.py:157
  106.2 129.6 %all-to-all-done.1 = f32[2,128,2,1536]{3,2,0,1:T(2,128)S(1)} async-done(((f32[2,128,2,1536]{3,2,0,1:T(2,128)}), f32[2,128,2,1536]{3,2,0,1:T(2,128)S(1)}, u32[]{:S(2)}, u32[]{:S(2)}) %all-to-all-start.1) | async-done | bytes 3145760 | tf_op jit(solution)/shard_map/all_to_all | solution.py:61
  235.8 1.6 copy.56
  237.4 2.3 fusion.154
  240.4 2.8 fusion.37
  243.2 2.5 copy.29
  245.7 1.7 fusion.35
  247.4 1.7 fusion.1
  249.2 1.7 fusion.2
  251.3 1.7 fusion.5
  252.9 1.7 fusion.4
  254.6 1.7 convolution_add_fusion
  256.3 2.1 subtract_bitcast_fusion
  258.7 3.6 copy.32
  262.2 150.9 %all_to_all.44 = f32[2,2,128,1536]{3,1,0,2:T(2,128)S(1)} all-to-all(f32[2,2,128,1536]{3,1,0,2:T(2,128)} %copy.32), channel_id=1, replica_groups=mesh['seq'=64,'chan'=8] {'seq'}, dimensions={2} | all-to-all | bytes 6291456 | tf_op jit(solution)/shard_map/all_to_all | solution.py:95
  420.4 49.5 %all_to_all.45 = f32[64,2,1536]{2,1,0:T(2,128)S(1)} all-to-all(f32[64,2,1536]{2,1,0:T(2,128)S(1)} %reshape.198), channel_id=1, replica_groups=mesh['seq'=64,'chan'=8] {'seq'}, dimensions={0} | all-to-all | bytes 1572864 | tf_op jit(solution)/shard_map/all_to_all | solution.py:107
  474.3 101.9 %psum.15 = f32[64]{0:T(128)S(1)} all-reduce(f32[64]{0:T(128)S(1)} %fusion.3), channel_id=1, replica_groups=mesh['seq'=64,'chan'=8] {'seq','chan'}, use_global_device_ids=true, to_apply=%region_2.3 | all-reduce | flops 64 | bytes 512 | tf_op jit(solution)/shard_map/psum | solution.py:158
  577.5 152.6 %all-reduce.2.cloned.1.call-done = f32[64,512]{1,0:T(8,128)} async-done(((f32[64,512]{1,0:T(8,128)}), f32[64,512]{1,0:T(8,128)}) %all-reduce.2.cloned.1.call-update) | async-done | bytes 131088 | tf_op jit(solution)/shard_map/psum | solution.py:157
  (78 shorter events, 26.3 us)
Async XLA Ops:
  7.2 5.8 copy-start
  7.9 6.5 collective-permute-start
  11.8 4.9 copy-start.6
  11.8 4.9 copy-start.8
  11.8 4.9 copy-start.10
  11.8 4.9 copy-start.12
  13.0 3.7 copy-start.4
  18.1 60.0 %all-to-all-start = ((f32[64,2,1536]{2,1,0:T(2,128)}), f32[64,2,1536]{2,1,0:T(2,128)S(1)}, u32[]{:S(2)}, u32[]{:S(2)}) async-start(f32[64,2,1536]{2,1,0:T(2,128)} %reshape.196), calls=%async_computation | async-start | bytes 1572864 | tf_op jit(solution)/shard_map/all_to_all | solution.py:46
  36.9 0.5 copy-start.17
  85.8 150.0 %all-to-all-start.1 = ((f32[2,128,2,1536]{3,2,0,1:T(2,128)}), f32[2,128,2,1536]{3,2,0,1:T(2,128)S(1)}, u32[]{:S(2)}, u32[]{:S(2)}) async-start(f32[2,128,2,1536]{3,2,0,1:T(2,128)} %copy.26), calls=%async_computation.1 | async-start | bytes 6291456 | tf_op jit(solution)/shard_map/all_to_all | solution.py:61
  92.9 637.2 %all-reduce.2.cloned.1.call-start = ((), (), s32[]{:S(2)}) async-start(), calls=%async_computation.4 | async-start | bytes 262144 | tf_op jit(solution)/shard_map/psum | solution.py:157
  245.7 1.7 copy-start.1
  254.6 1.7 copy-start.14
  254.6 1.7 copy-start.15
  420.3 50.2 %copy-start.5 = (f32[64]{0:T(128)S(1)}, f32[64]{0:T(128)}, u32[]{:S(2)}) copy-start(f32[64]{0:T(128)} %copy-done.4) | copy-start | bytes 772
  420.4 50.2 %copy-start.7 = (f32[128]{0:T(128)S(1)}, f32[128]{0:T(128)}, u32[]{:S(2)}) copy-start(f32[128]{0:T(128)} %copy-done.6) | copy-start | bytes 1540
  420.4 50.2 %copy-start.9 = (s32[128]{0:T(128)S(1)}, s32[128]{0:T(128)}, u32[]{:S(2)}) copy-start(s32[128]{0:T(128)} %copy-done.8) | copy-start | bytes 1540
  420.4 50.2 %copy-start.11 = (pred[64]{0:T(512)(128)(4,1)S(1)}, pred[64]{0:T(512)(128)(4,1)}, u32[]{:S(2)}) copy-start(pred[64]{0:T(512)(128)(4,1)} %copy-done.10) | copy-start | bytes 196
  420.4 50.2 %copy-start.13 = (s32[64]{0:T(128)S(1)}, s32[64]{0:T(128)}, u32[]{:S(2)}) copy-start(s32[64]{0:T(128)} %copy-done.12) | copy-start | bytes 772
  420.4 51.3 %copy-start.2 = (bf16[128,512]{1,0:T(8,128)(2,1)S(1)}, bf16[128,512]{1,0:T(8,128)(2,1)}, u32[]{:S(2)}) copy-start(bf16[128,512]{1,0:T(8,128)(2,1)} %param.7) | copy-start | bytes 393220
  420.4 51.3 %copy-start.3 = (bf16[128,512]{1,0:T(8,128)(2,1)S(1)}, bf16[128,512]{1,0:T(8,128)(2,1)}, u32[]{:S(2)}) copy-start(bf16[128,512]{1,0:T(8,128)(2,1)} %param.8) | copy-start | bytes 393220
  469.9 3.9 copy-start.16
  472.5 104.3 %collective-permute-start.1 = (f32[2,512]{1,0:T(2,128)S(1)}, f32[2,512]{1,0:T(2,128)S(1)}, u32[]{:S(2)}, u32[]{:S(2)}) collective-permute-start(f32[2,512]{1,0:T(2,128)S(1)} %slice.116), channel_id=1, source_target_pairs={{8,0},{16,8},{24,16},{32,24},{40,32},{48,40},{56,48},{64,56},{72,6... | collective-permute-start | bytes 12296 | tf_op jit(solution)/shard_map/ppermute | solution.py:13
Sparse Core Ops, SparseCore 0:
  473.9 256.1 all-reduce.1
where the time goes:
time: 746 us; the launch traced here: 739 us
  waiting for transfers between devices  323 us (43%)
  blocking collectives  302 us (40%)
  starting transfers between devices  42.9 us (6%)
  local copies, waits for them, and re-layouts  25.4 us (3%)
  matrix products  22.9 us (3%)
  between operations  15 us (2%)
  other arithmetic  7.67 us (1%)
    psum x1, waiting for transfers between devices, per_device(): grad_coef = lax.psum(coef_part, 'seq')  153 us
    all_to_all x1, blocking collectives, inverse_transform(): lax.all_to_all(jnp.stack([real_c, imag_c]), 'seq', split_axis=2, concat_a...  151 us
    all_to_all x1, waiting for transfers between devices, forward_transform(): lax.all_to_all(jnp.stack([real_b, imag_b]), 'seq', split_axis=1, concat_a...  130 us
    psum x1, blocking collectives, per_device(): rate_sum = lax.psum(rate_part, ('seq', 'chan'))  102 us
    all_to_all x1, blocking collectives, inverse_transform(): lax.all_to_all(signal.reshape(shards, slab, width), 'seq', split_axis=0,...  49.5 us
    all_to_all x1, waiting for transfers between devices, forward_transform(): lax.all_to_all(columns.reshape(shards, slab, width), 'seq', split_axis=0,...  40.5 us
    all_to_all x1, starting transfers between devices, forward_transform(): lax.all_to_all(columns.reshape(shards, slab, width), 'seq', split_axis=0,...  18.9 us
  transfers between devices with their start and end apart: 5, of which 3 were waited for; matrix products, arithmetic and copies ran while one was open for 1% of the time, Pallas kernels for 0%

commit v1 on v0

--- a/solution.py
+++ b/solution.py
@@ -155,7 +155,7 @@
     coef_part = jnp.dot(phi.T, grad_filter, precision=highest) * length ** (-0.5)
     rate_part = jnp.sum(psi * jnp.dot(grad_filter, coef.T, precision=highest), axis=0)
     grad_coef = lax.psum(coef_part, "seq")
-    rate_sum = lax.psum(rate_part, ("seq", "chan"))
+    rate_sum = jnp.sum(lax.all_gather(rate_part, ("seq", "chan")), axis=0)
     grad_rate = rate_sum * (length * chans * lax.axis_size("chan")) ** (-0.5)
     out_y = (second * conv).astype(jnp.bfloat16)
     grad_x1 = (grad_gated * mixed).astype(jnp.bfloat16)

time: 746 us -> 1200 us (1.61)
  waiting for transfers between devices: 323 us -> 921 us
  blocking collectives: 302 us -> 151 us
    unnamed x1 -> x3, waiting for transfers between devices: 0.02 us -> 439 us
    psum x1, waiting for transfers between devices: 153 us -> 255 us  [per_device(): grad_coef = lax.psum(coef_part, 'seq')]
    psum x1 -> x0, blocking collectives: 102 us -> none  [per_device(): rate_sum = lax.psum(rate_part, ('seq', 'chan'))]
    all_to_all x1 -> x0, blocking collectives: 49.5 us -> none  [inverse_transform(): lax.all_to_all(signal.reshape(shards, slab, width), 'seq', split_axis=0,...]
    all_to_all x0 -> x1, waiting for transfers between devices: none -> 42.8 us  [inverse_transform(): lax.all_to_all(signal.reshape(shards, slab, width), 'seq', split_axis=0,...]
  transfers between devices with their start and end apart: 5 -> 7, of which waited for: 3 -> 6; matrix products, arithmetic and copies ran while one was open for 1% -> 1% of each run, Pallas kernels for 0% -> 0%
where the time goes in v1:
time: 1200 us; the launch traced here: 1190 us
  waiting for transfers between devices  921 us (77%)
  blocking collectives  151 us (13%)
  starting transfers between devices  49.7 us (4%)
  local copies, waits for them, and re-layouts  27.7 us (2%)
  matrix products  22.9 us (2%)
  between operations  15 us (1%)
    unnamed x3, waiting for transfers between devices  439 us
    psum x1, waiting for transfers between devices, per_device(): grad_coef = lax.psum(coef_part, 'seq')  255 us
    all_to_all x1, blocking collectives, inverse_transform(): lax.all_to_all(jnp.stack([real_c, imag_c]), 'seq', split_axis=2, concat_a...  151 us
    all_to_all x1, waiting for transfers between devices, forward_transform(): lax.all_to_all(jnp.stack([real_b, imag_b]), 'seq', split_axis=1, concat_a...  141 us
    all_to_all x1, waiting for transfers between devices, inverse_transform(): lax.all_to_all(signal.reshape(shards, slab, width), 'seq', split_axis=0,...  42.8 us
    all_to_all x1, waiting for transfers between devices, forward_transform(): lax.all_to_all(columns.reshape(shards, slab, width), 'seq', split_axis=0,...  41 us
  transfers between devices with their start and end apart: 7, of which 6 were waited for; matrix products, arithmetic and copies ran while one was open for 1% of the time, Pallas kernels for 0%

profile of v1, /device:TPU:2, one launch (start us, length us, event | category | flops | bytes accessed | tf_op | source)
XLA Modules:
  0.0 1194.7 jit_solution(2344057409374398228)
XLA Ops:
  7.9 3.8 collective-permute-start
  18.1 18.9 %all-to-all-start = ((f32[64,2,1536]{2,1,0:T(2,128)}), f32[64,2,1536]{2,1,0:T(2,128)S(1)}, u32[]{:S(2)}, u32[]{:S(2)}) async-start(f32[64,2,1536]{2,1,0:T(2,128)} %reshape.196), calls=%async_computation | async-start | bytes 1572864 | tf_op jit(solution)/shard_map/all_to_all | solution.py:46
  37.1 41.0 %all-to-all-done = f32[64,2,1536]{2,1,0:T(2,128)S(1)} async-done(((f32[64,2,1536]{2,1,0:T(2,128)}), f32[64,2,1536]{2,1,0:T(2,128)S(1)}, u32[]{:S(2)}, u32[]{:S(2)}) %all-to-all-start) | async-done | bytes 786464 | tf_op jit(solution)/shard_map/all_to_all | solution.py:46
  79.7 1.9 add_bitcast_fusion.1
  81.8 4.1 copy.26
  85.8 18.9 %all-to-all-start.1 = ((f32[2,128,2,1536]{3,2,0,1:T(2,128)}), f32[2,128,2,1536]{3,2,0,1:T(2,128)S(1)}, u32[]{:S(2)}, u32[]{:S(2)}) async-start(f32[2,128,2,1536]{3,2,0,1:T(2,128)} %copy.26), calls=%async_computation.1 | async-start | bytes 6291456 | tf_op jit(solution)/shard_map/all_to_all | solution.py:61
  106.1 141.3 %all-to-all-done.1 = f32[2,128,2,1536]{3,2,0,1:T(2,128)S(1)} async-done(((f32[2,128,2,1536]{3,2,0,1:T(2,128)}), f32[2,128,2,1536]{3,2,0,1:T(2,128)S(1)}, u32[]{:S(2)}, u32[]{:S(2)}) %all-to-all-start.1) | async-done | bytes 3145760 | tf_op jit(solution)/shard_map/all_to_all | solution.py:61
  247.4 1.6 copy.56
  249.0 2.3 fusion.154
  252.0 2.8 fusion.37
  254.8 2.5 copy.29
  257.3 1.7 fusion.35
  259.0 1.7 fusion.1
  260.8 1.7 fusion.2
  262.9 1.7 fusion.5
  264.6 1.7 fusion.4
  266.3 1.7 convolution_add_fusion
  268.0 2.1 subtract_bitcast_fusion
  270.4 3.6 copy.32
  273.9 150.9 %all_to_all.44 = f32[2,2,128,1536]{3,1,0,2:T(2,128)S(1)} all-to-all(f32[2,2,128,1536]{3,1,0,2:T(2,128)} %copy.32), channel_id=1, replica_groups=mesh['seq'=64,'chan'=8] {'seq'}, dimensions={2} | all-to-all | bytes 6291456 | tf_op jit(solution)/shard_map/all_to_all | solution.py:95
  433.0 6.8 all-to-all-start.3
  439.9 42.8 %all-to-all-done.3 = f32[64,2,1536]{2,1,0:T(2,128)S(1)} async-done(((f32[64,2,1536]{2,1,0:T(2,128)}), f32[64,2,1536]{2,1,0:T(2,128)S(1)}, u32[]{:S(2)}, u32[]{:S(2)}) %all-to-all-start.3) | async-done | bytes 786464 | tf_op jit(solution)/shard_map/all_to_all | solution.py:107
  490.3 438.7 %all-reduce.6.cloned.1.call-done = f32[32768]{0:T(1024)} async-done(((f32[32768]{0:T(1024)}), f32[32768]{0:T(1024)}) %all-reduce.6.cloned.1.call-update) | async-done | bytes 131088
  930.6 255.3 %all-reduce.4.cloned.1.call-done = f32[64,512]{1,0:T(8,128)} async-done(((f32[64,512]{1,0:T(8,128)}), f32[64,512]{1,0:T(8,128)}) %all-reduce.4.cloned.1.call-update) | async-done | bytes 131088 | tf_op jit(solution)/shard_map/psum | solution.py:157
  (87 shorter events, 30.3 us)
Async XLA Ops:
  7.2 5.8 copy-start
  7.9 6.5 collective-permute-start
  11.8 3.7 copy-start.7
  11.8 3.6 copy-start.9
  11.8 3.6 copy-start.11
  11.8 3.6 copy-start.13
  13.0 2.4 copy-start.5
  18.1 60.0 %all-to-all-start = ((f32[64,2,1536]{2,1,0:T(2,128)}), f32[64,2,1536]{2,1,0:T(2,128)S(1)}, u32[]{:S(2)}, u32[]{:S(2)}) async-start(f32[64,2,1536]{2,1,0:T(2,128)} %reshape.196), calls=%async_computation | async-start | bytes 1572864 | tf_op jit(solution)/shard_map/all_to_all | solution.py:46
  36.9 44.6 %copy-start.18 = (s32[2]{0:T(128)}, s32[2]{0:T(128)S(1)}, u32[]{:S(2)}) copy-start(s32[2]{0:T(128)S(1)} %iota_add_fusion) | copy-start | bytes 28
  85.8 161.6 %all-to-all-start.1 = ((f32[2,128,2,1536]{3,2,0,1:T(2,128)}), f32[2,128,2,1536]{3,2,0,1:T(2,128)S(1)}, u32[]{:S(2)}, u32[]{:S(2)}) async-start(f32[2,128,2,1536]{3,2,0,1:T(2,128)} %copy.26), calls=%async_computation.1 | async-start | bytes 6291456 | tf_op jit(solution)/shard_map/all_to_all | solution.py:61
  266.3 1.8 copy-start.15
  266.3 1.8 copy-start.16
  433.0 50.3 %copy-start.2 = (bf16[128,512]{1,0:T(8,128)(2,1)S(1)}, bf16[128,512]{1,0:T(8,128)(2,1)}, u32[]{:S(2)}) copy-start(bf16[128,512]{1,0:T(8,128)(2,1)} %param.7) | copy-start | bytes 393220
  433.0 50.3 %copy-start.3 = (bf16[128,512]{1,0:T(8,128)(2,1)S(1)}, bf16[128,512]{1,0:T(8,128)(2,1)}, u32[]{:S(2)}) copy-start(bf16[128,512]{1,0:T(8,128)(2,1)} %param.8) | copy-start | bytes 393220
  433.0 49.7 %all-to-all-start.3 = ((f32[64,2,1536]{2,1,0:T(2,128)}), f32[64,2,1536]{2,1,0:T(2,128)S(1)}, u32[]{:S(2)}, u32[]{:S(2)}) async-start(f32[64,2,1536]{2,1,0:T(2,128)} %reshape.198), calls=%async_computation.3 | async-start | bytes 1572864 | tf_op jit(solution)/shard_map/all_to_all | solution.py:107
  439.8 489.2 %all-reduce.6.cloned.1.call-start = ((), (), s32[]{:S(2)}) async-start(), calls=%async_computation.5 | async-start | bytes 262144
  439.8 45.6 %copy-start.6 = (f32[64]{0:T(128)S(1)}, f32[64]{0:T(128)}, u32[]{:S(2)}) copy-start(f32[64]{0:T(128)} %copy-done.5) | copy-start | bytes 772
  439.8 45.6 %copy-start.8 = (f32[128]{0:T(128)S(1)}, f32[128]{0:T(128)}, u32[]{:S(2)}) copy-start(f32[128]{0:T(128)} %copy-done.7) | copy-start | bytes 1540
  439.8 45.6 %copy-start.10 = (s32[128]{0:T(128)S(1)}, s32[128]{0:T(128)}, u32[]{:S(2)}) copy-start(s32[128]{0:T(128)} %copy-done.9) | copy-start | bytes 1540
  439.8 45.6 %copy-start.12 = (pred[64]{0:T(512)(128)(4,1)S(1)}, pred[64]{0:T(512)(128)(4,1)}, u32[]{:S(2)}) copy-start(pred[64]{0:T(512)(128)(4,1)} %copy-done.11) | copy-start | bytes 196
  439.9 45.6 %copy-start.14 = (s32[64]{0:T(128)S(1)}, s32[64]{0:T(128)}, u32[]{:S(2)}) copy-start(s32[64]{0:T(128)} %copy-done.13) | copy-start | bytes 772
  439.9 45.6 %copy-start.17 = (f32[64]{0:T(128)S(1)}, f32[64]{0:T(128)}, u32[]{:S(2)}) copy-start(f32[64]{0:T(128)} %get-tuple-element.27) | copy-start | bytes 772
  484.1 5.5 collective-permute-start.1
  486.9 699.0 %all-reduce.4.cloned.1.call-start = ((), (), s32[]{:S(2)}) async-start(), calls=%async_computation.4 | async-start | bytes 262144 | tf_op jit(solution)/shard_map/psum | solution.py:157
  (2 other events, 2.4 us)
Sparse Core Ops, SparseCore 0:
  487.0 441.9 all-reduce.5
  933.3 252.5 all-reduce.3
